TPU v7x, 128 devices: a whole 4x4x4 slice. The times are simulated.
128 devices in a mesh: dp: 2 (over z_hi), expert: 64 (over z_lo, y, x, core).
Axes of the slice: x: 4, y: 4, z: 4 (z_hi: 2, z_lo: 2; z = z_hi * 2 + z_lo), core: 2. Of those that a mesh axis runs over, the one named last changes fastest.
Arguments:
- tokens: bfloat16 [8192, 3584], P(('dp', 'expert')), may hold values from -6 to 6
- expert_ids: int32 [8192, 8], P(('dp', 'expert')), may hold values from 0 to 63, all different within a row; in each aligned block of 64 rows (0 to 63, 64 to 127, ...) at most 16 rows name the same one
- router_weight: bfloat16 [3584, 64], replicated, may hold values from -0.09375 to 0.09375
- gate_weight: bfloat16 [64, 3584, 1024], P('expert'), may hold values from -0.09375 to 0.09375
- up_weight: bfloat16 [64, 3584, 1024], P('expert'), may hold values from -0.09375 to 0.09375
- down_weight: bfloat16 [64, 1024, 3584], P('expert'), may hold values from -0.1875 to 0.1875
Outputs:
- mixed: bfloat16 [8192, 3584], P(('dp', 'expert'))
- load_ratio: float32 [64], replicated
Inputs may be any that keep to these rules, and one draw needn't show every extreme that they name: `expert_ids`: each row names 8 different experts; among the rows of one device no expert is named by more than 16 rows, a bound that some block reaches.
All inputs are finite; a program needn't handle non-finite values.
Results may differ from a plain program's by a relative error of at most 0.0058.
Values may be sent and summed in bfloat16 or wider, within the bound.
A program may use at most 192 MiB of HBM per device.

v0:
```python
import functools

import jax
import jax.numpy as jnp
from jax import lax
from jax.experimental import pallas as pl
from jax.experimental.pallas import tpu as pltpu
from jax.sharding import PartitionSpec as P

MESH = pl.DeviceIdType.MESH
CAP = 16
NEAR = 8


def moe_kernel(
    sizes,
    tokens_ref, ids_ref, router_ref, wg_hbm, wu_hbm, wd_hbm,
    mixed_ref, load_ref,
    wg, wu, wd, gathered, routes, packed, served, back, sums, hidden, route, tally, tallies, twin,
    w_sem, g_send, g_recv, r_send, r_recv, d_send, d_recv, t_send, t_recv, p_send, p_recv,
    c_send, c_recv, x_send, x_recv,
):
    rows, depth, width, experts, top = sizes
    f32, bf16 = jnp.float32, jnp.bfloat16
    dp, me = lax.axis_index("dp"), lax.axis_index("expert")
    c = me % 2
    x = (me // 2) % 4
    y = (me // 8) % 4
    z = me // 32
    g = (1 - c) * y + c * x
    h = (1 - c) * x + c * y
    g_step, h_step = 8 - 6 * c, 2 + 6 * c
    my_place = h * 2 + c
    my_source = c * 4 + h
    slot_rows = 2 * CAP

    def offset_of(m):
        return m + (m // 2) * (1 - 2 * (m % 2))

    def chunk_there(m):
        return (m % 2) * 2 + m // 2

    def plane_device(m, q):
        return (z + q - 2 * z * q) * 32 + ((g + offset_of(m)) % 4) * g_step + h * h_step + c

    def served_device(place):
        return z * 32 + g * g_step + (place // 2) * h_step + place % 2

    def source_device(source):
        kind, far = source // 4, source % 4
        return z * 32 + (1 - kind) * (y * 8 + far * 2) + kind * (far * 8 + x * 2 + 1)

    def place_there(source):
        kind = source // 4
        return ((1 - kind) * x + kind * y) * 2 + c

    def rows_of(index):
        return pl.ds(pl.multiple_of(index * slot_rows, slot_rows), slot_rows)

    barrier = pltpu.get_barrier_semaphore()

    def greet(device):
        pl.semaphore_signal(barrier, inc=1, device_id=device, device_id_type=MESH)

    for i in range(1, NEAR):
        greet((dp, plane_device(i // 2, i % 2)))

    def greet_sets(k, carry):
        greet((dp, served_device((my_place + k) % NEAR)))
        greet((dp, source_device((my_source + k) % NEAR)))
        return carry

    lax.fori_loop(1, NEAR, greet_sets, 0)
    greet((1 - dp, me))

    weights = [
        pltpu.make_async_copy(wg_hbm.at[0], wg, w_sem.at[0]),
        pltpu.make_async_copy(wu_hbm.at[0], wu, w_sem.at[1]),
        pltpu.make_async_copy(wd_hbm.at[0], wd, w_sem.at[2]),
    ]
    for copy in weights:
        copy.start()

    token_block = tokens_ref[...]
    logits = jnp.dot(token_block, router_ref[...], preferred_element_type=f32)
    lane = lax.broadcasted_iota(jnp.int32, (rows, experts), 1)
    chosen = jnp.zeros((rows, experts), f32)
    for k in range(top):
        chosen = jnp.where(ids_ref[:, k : k + 1] == lane, 1.0, chosen)
    affinity = jnp.where(chosen > 0, 1.0 / (1.0 + jnp.exp(-logits)), 0.0)
    gates = 2.5 * affinity / jnp.sum(affinity, axis=1, keepdims=True)
    later = lax.broadcasted_iota(jnp.int32, (rows, rows), 0)
    earlier = lax.broadcasted_iota(jnp.int32, (rows, rows), 1)
    upto = jnp.where(earlier <= later, 1.0, 0.0).astype(bf16)
    ranks = jnp.dot(upto, chosen.astype(bf16), preferred_element_type=f32)
    both = jnp.concatenate([chosen * ranks, gates], axis=1)
    route[...] = jnp.concatenate([both, both], axis=0).T
    gathered[0, 0:rows, :] = token_block
    routes[0, 0] = route[...]

    pl.semaphore_wait(barrier, 3 * (NEAR - 1) + 1)

    def token_copy(i):
        m, q = i // 2, i % 2
        slot = chunk_there(m)
        return pltpu.make_async_remote_copy(
            src_ref=tokens_ref,
            dst_ref=gathered.at[slot, pl.ds(q * rows, rows)],
            send_sem=g_send.at[i],
            recv_sem=g_recv.at[slot * 2 + q],
            device_id=(dp, plane_device(m, q)),
            device_id_type=MESH,
        )

    def route_copy(i):
        m, q = i // 2, i % 2
        slot = chunk_there(m)
        return pltpu.make_async_remote_copy(
            src_ref=route,
            dst_ref=routes.at[slot, q],
            send_sem=r_send.at[i],
            recv_sem=r_recv.at[slot * 2 + q],
            device_id=(dp, plane_device(m, q)),
            device_id_type=MESH,
        )

    for i in range(1, NEAR):
        token_copy(i).start()
        route_copy(i).start()

    def landed(ref, sem):
        pltpu.make_async_copy(ref, ref, sem).wait()

    def wait_block(m, q):
        landed(gathered.at[m, pl.ds(q * rows, rows)], g_recv.at[m * 2 + q])
        landed(routes.at[m, q], r_recv.at[m * 2 + q])

    def spread(m, base):
        first_half = lax.broadcasted_iota(jnp.int32, (1, 2 * rows), 1) < rows
        bands = []
        for place in range(NEAR):
            expert = base + served_device(place)
            row = jnp.where(
                first_half, routes[m, 0, pl.ds(expert, 1), :], routes[m, 1, pl.ds(expert, 1), :]
            )
            bands.append(jnp.broadcast_to(row, (slot_rows, 2 * rows)))
        return jnp.concatenate(bands, axis=0)

    def taken(m):
        slot = lax.broadcasted_iota(jnp.int32, (NEAR * slot_rows, 2 * rows), 0) % slot_rows
        block = lax.broadcasted_iota(jnp.int32, (NEAR * slot_rows, 2 * rows), 1) // rows
        wanted = jnp.where(slot // CAP == block, slot % CAP + 1, -1).astype(f32)
        return spread(m, 0) == wanted

    def pack_chunk(m):
        select = jnp.where(taken(m), 1.0, 0.0).astype(bf16)

        def tile(n, carry):
            columns = pl.ds(pl.multiple_of(n * 512, 512), 512)
            packed[m, :, columns] = jnp.dot(
                select, gathered[m, :, columns], preferred_element_type=f32
            ).astype(bf16)
            return carry

        lax.fori_loop(0, depth // 512, tile, 0)

    def hand_out(m, k):
        place = (my_place + k) % NEAR
        return pltpu.make_async_remote_copy(
            src_ref=packed.at[m, rows_of(place)],
            dst_ref=served.at[m, rows_of(my_source)],
            send_sem=d_send.at[m * NEAR + k],
            recv_sem=d_recv.at[m * NEAR + my_source],
            device_id=(dp, served_device(place)),
            device_id_type=MESH,
        )

    def pack_and_send(m, carry):
        @pl.when(m > 0)
        def _():
            wait_block(m, 0)

        wait_block(m, 1)
        pack_chunk(m)

        def send(k, carry):
            hand_out(m, k).start()
            return carry

        lax.fori_loop(1, NEAR, send, 0)
        pltpu.make_async_copy(
            packed.at[m, rows_of(my_place)],
            served.at[m, rows_of(my_source)],
            d_recv.at[m * NEAR + my_source],
        ).start()
        return carry

    lax.fori_loop(0, 4, pack_and_send, 0)

    plane = jnp.zeros((experts, 2 * rows), f32)
    for i in range(NEAR):
        plane = plane + jnp.where(routes[i // 2, i % 2, 0:experts, :] > 0, 0.5, 0.0)
    tally[...] = plane

    def tally_copy(k):
        return pltpu.make_async_remote_copy(
            src_ref=tally,
            dst_ref=tallies.at[my_source],
            send_sem=c_send.at[k],
            recv_sem=c_recv.at[my_source],
            device_id=(dp, served_device((my_place + k) % NEAR)),
            device_id_type=MESH,
        )

    def send_tally(k, carry):
        tally_copy(k).start()
        return carry

    lax.fori_loop(1, NEAR, send_tally, 0)
    pltpu.make_async_copy(tally, tallies.at[my_source], c_recv.at[my_source]).start()

    for copy in weights:
        copy.wait()

    def hand_back(m, k):
        source = (my_source + k) % NEAR
        place = place_there(source)
        return pltpu.make_async_remote_copy(
            src_ref=served.at[m, rows_of(source)],
            dst_ref=back.at[m, rows_of(place)],
            send_sem=t_send.at[m * NEAR + k],
            recv_sem=t_recv.at[m * NEAR + place],
            device_id=(dp, source_device(source)),
            device_id_type=MESH,
        )

    def serve(m, carry):
        def arrive(source, carry):
            landed(served.at[m, rows_of(source)], d_recv.at[m * NEAR + source])
            return carry

        lax.fori_loop(0, NEAR, arrive, 0)

        def into_hidden(n, carry):
            columns = pl.ds(pl.multiple_of(n * 256, 256), 256)
            gate_part = jnp.dot(served[m], wg[:, columns], preferred_element_type=f32)
            up_part = jnp.dot(served[m], wu[:, columns], preferred_element_type=f32)
            act = gate_part / (1.0 + jnp.exp(-gate_part)) * up_part
            hidden[:, columns] = act.astype(bf16)
            return carry

        lax.fori_loop(0, width // 256, into_hidden, 0)

        def out_of_hidden(n, carry):
            columns = pl.ds(pl.multiple_of(n * 512, 512), 512)
            served[m, :, columns] = jnp.dot(
                hidden[...], wd[:, columns], preferred_element_type=f32
            ).astype(bf16)
            return carry

        lax.fori_loop(0, depth // 512, out_of_hidden, 0)

        def send(k, carry):
            hand_back(m, k).start()
            return carry

        lax.fori_loop(1, NEAR, send, 0)
        pltpu.make_async_copy(
            served.at[m, rows_of(my_source)],
            back.at[m, rows_of(my_place)],
            t_recv.at[m * NEAR + my_place],
        ).start()
        return carry

    lax.fori_loop(0, 4, serve, 0)

    group = jnp.zeros((experts, 2 * rows), f32)
    for source in range(NEAR):
        landed(tallies.at[source], c_recv.at[source])
        group = group + tallies[source]
    twin[0] = group
    twin_copy = pltpu.make_async_remote_copy(
        src_ref=twin.at[0],
        dst_ref=twin.at[1],
        send_sem=x_send,
        recv_sem=x_recv,
        device_id=(1 - dp, me),
        device_id_type=MESH,
    )
    twin_copy.start()

    def sum_copy(m, q):
        slot = chunk_there(m)
        return pltpu.make_async_remote_copy(
            src_ref=gathered.at[m, pl.ds(q * rows, rows)],
            dst_ref=sums.at[slot * 2 + q],
            send_sem=p_send.at[m * 2 + q],
            recv_sem=p_recv.at[slot * 2 + q],
            device_id=(dp, plane_device(m, q)),
            device_id_type=MESH,
        )

    def combine(m, carry):
        def arrive(place, carry):
            landed(back.at[m, rows_of(place)], t_recv.at[m * NEAR + place])
            return carry

        lax.fori_loop(0, NEAR, arrive, 0)
        weight = jnp.where(taken(m), spread(m, experts), 0.0).T
        high = weight.astype(bf16)
        low = (weight - high.astype(f32)).astype(bf16)

        def tile(n, carry):
            columns = pl.ds(pl.multiple_of(n * 512, 512), 512)
            block = back[m, :, columns]
            total = jnp.dot(high, block, preferred_element_type=f32)
            total = total + jnp.dot(low, block, preferred_element_type=f32)
            gathered[m, :, columns] = total.astype(bf16)
            return carry

        lax.fori_loop(0, depth // 512, tile, 0)

        @pl.when(m > 0)
        def _():
            sum_copy(m, 0).start()

        sum_copy(m, 1).start()
        return carry

    lax.fori_loop(0, 4, combine, 0)

    twin_copy.wait()
    pairs = (twin[0] + twin[1]) * (1.0 / 1024.0)
    load_ref[...] = jnp.sum(
        jnp.concatenate([pairs, jnp.zeros_like(pairs)], axis=0).T, axis=0, keepdims=True
    )

    for i in range(1, NEAR):
        landed(sums.at[i], p_recv.at[i])

    def finish(n, carry):
        columns = pl.ds(pl.multiple_of(n * 512, 512), 512)
        total = gathered[0, 0:rows, columns].astype(f32)
        for i in range(1, NEAR):
            total = total + sums[i, :, columns].astype(f32)
        mixed_ref[:, columns] = total.astype(bf16)
        return carry

    lax.fori_loop(0, depth // 512, finish, 0)

    for i in range(1, NEAR):
        token_copy(i).wait_send()
        route_copy(i).wait_send()
        sum_copy(i // 2, i % 2).wait_send()

    def sent(k, carry):
        tally_copy(k).wait_send()

        def sent_chunk(m, carry):
            hand_out(m, k).wait_send()
            hand_back(m, k).wait_send()
            return carry

        return lax.fori_loop(0, 4, sent_chunk, carry)

    lax.fori_loop(1, NEAR, sent, 0)


def local(tokens, expert_ids, router_weight, gate_weight, up_weight, down_weight):
    rows, depth = tokens.shape
    top = expert_ids.shape[1]
    experts = router_weight.shape[1]
    width = gate_weight.shape[2]
    bf16, f32 = jnp.bfloat16, jnp.float32
    slots = NEAR * 2 * CAP
    vmem = pl.BlockSpec(memory_space=pltpu.VMEM)
    hbm = pl.BlockSpec(memory_space=pl.ANY)
    dma = pltpu.SemaphoreType.DMA
    mixed, load = pl.pallas_call(
        functools.partial(moe_kernel, (rows, depth, width, experts, top)),
        out_shape=(
            jax.ShapeDtypeStruct((rows, depth), bf16),
            jax.ShapeDtypeStruct((1, 2 * experts), f32),
        ),
        in_specs=[vmem, vmem, vmem, hbm, hbm, hbm],
        out_specs=(vmem, vmem),
        scratch_shapes=[
            pltpu.VMEM((depth, width), bf16),
            pltpu.VMEM((depth, width), bf16),
            pltpu.VMEM((width, depth), bf16),
            pltpu.VMEM((4, 2 * rows, depth), bf16),
            pltpu.VMEM((4, 2, 2 * experts, 2 * rows), f32),
            pltpu.VMEM((4, slots, depth), bf16),
            pltpu.VMEM((4, slots, depth), bf16),
            pltpu.VMEM((4, slots, depth), bf16),
            pltpu.VMEM((NEAR, rows, depth), bf16),
            pltpu.VMEM((slots, width), bf16),
            pltpu.VMEM((2 * experts, 2 * rows), f32),
            pltpu.VMEM((experts, 2 * rows), f32),
            pltpu.VMEM((NEAR, experts, 2 * rows), f32),
            pltpu.VMEM((2, experts, 2 * rows), f32),
            dma((3,)),
            dma((NEAR,)), dma((NEAR,)),
            dma((NEAR,)), dma((NEAR,)),
            dma((4 * NEAR,)), dma((4 * NEAR,)),
            dma((4 * NEAR,)), dma((4 * NEAR,)),
            dma((NEAR,)), dma((NEAR,)),
            dma((NEAR,)), dma((NEAR,)),
            dma, dma,
        ],
        compiler_params=pltpu.CompilerParams(
            collective_id=0, has_side_effects=True, vmem_limit_bytes=60 * 1024 * 1024
        ),
    )(tokens, expert_ids, router_weight, gate_weight, up_weight, down_weight)
    return mixed, load[0, :experts]


def solution(mesh):
    return jax.shard_map(
        local,
        mesh=mesh,
        in_specs=(
            P(("dp", "expert"), None),
            P(("dp", "expert"), None),
            P(),
            P("expert", None, None),
            P("expert", None, None),
            P("expert", None, None),
        ),
        out_specs=(P(("dp", "expert"), None), P()),
        check_vma=False,
    )
```

profile of v0, /device:TPU:1, one launch (start us, length us, event | category | flops | bytes accessed | tf_op | source)
XLA Modules:
  0.0 182.2 jit_solution(10198021517573806764)
XLA Ops:
  0.6 1.4 copy.8.ids_ref
  2.0 2.3 %copy.9.router_ref = bf16[3584,64]{1,0:T(8,128)(2,1)} copy(bf16[3584,64]{0,1:T(8,128)(2,1)} %param.8) | data formatting | bytes 917504 | tf_op args[2]
  4.3 174.9 %shard_map.77 = (bf16[64,3584]{1,0:T(8,128)(2,1)}, f32[1,128]{1,0:T(1,128)}) custom-call(bf16[64,3584]{1,0:T(8,128)(2,1)} %tokens_ref.1, s32[64,8]{1,0:T(8,128)} %copy.8.ids_ref, bf16[3584,64]{1,0:T(8,128)(2,1)} %copy.9.router_ref, bf16[1,3584,1024]{2,1,0:T(8,128)(2,1)} %wg_hbm.1, bf16[1,3584,1024]{2,1,0:T(8,128)(2,1)} %wu_hbm.1, bf16[1,1024,3584]{2,1,0:T(8,128)(2,1)} %wd_hbm.1), custom_call_target="tpu_custom_call" | custom-call | tf_op jit(solution)/shard_map/pallas_call | solution.py:379
  179.2 1.2 slice_bitcast_fusion
  180.4 1.8 copy.11
where the time goes:
time: 185 us; the launch traced here: 182 us
  Pallas kernels  175 us (95%)
  local copies, waits for them, and re-layouts  6.64 us (4%)
    pallas_call x1, Pallas kernels, local(): pl.pallas_call(functools.partial(moe_kernel, (rows, depth, width, experts...  175 us
    unnamed x3, local copies, waits for them, and re-layouts  5.46 us

commit v1 on v0

--- a/solution.py
+++ b/solution.py
@@ -81,34 +81,19 @@
     for copy in weights:
         copy.start()
 
-    token_block = tokens_ref[...]
-    logits = jnp.dot(token_block, router_ref[...], preferred_element_type=f32)
-    lane = lax.broadcasted_iota(jnp.int32, (rows, experts), 1)
-    chosen = jnp.zeros((rows, experts), f32)
-    for k in range(top):
-        chosen = jnp.where(ids_ref[:, k : k + 1] == lane, 1.0, chosen)
-    affinity = jnp.where(chosen > 0, 1.0 / (1.0 + jnp.exp(-logits)), 0.0)
-    gates = 2.5 * affinity / jnp.sum(affinity, axis=1, keepdims=True)
-    later = lax.broadcasted_iota(jnp.int32, (rows, rows), 0)
-    earlier = lax.broadcasted_iota(jnp.int32, (rows, rows), 1)
-    upto = jnp.where(earlier <= later, 1.0, 0.0).astype(bf16)
-    ranks = jnp.dot(upto, chosen.astype(bf16), preferred_element_type=f32)
-    both = jnp.concatenate([chosen * ranks, gates], axis=1)
-    route[...] = jnp.concatenate([both, both], axis=0).T
-    gathered[0, 0:rows, :] = token_block
-    routes[0, 0] = route[...]
-
+    gathered[0, 0:rows, :] = tokens_ref[...]
     pl.semaphore_wait(barrier, 3 * (NEAR - 1) + 1)
 
     def token_copy(i):
         m, q = i // 2, i % 2
         slot = chunk_there(m)
-        return pltpu.make_async_remote_copy(
-            src_ref=tokens_ref,
+        relayed = m > 0 and q == 1
+        return pltpu.make_async_remote_copy(
+            src_ref=gathered.at[0, pl.ds(rows, rows)] if relayed else tokens_ref,
             dst_ref=gathered.at[slot, pl.ds(q * rows, rows)],
             send_sem=g_send.at[i],
             recv_sem=g_recv.at[slot * 2 + q],
-            device_id=(dp, plane_device(m, q)),
+            device_id=(dp, plane_device(m, 0 if relayed else q)),
             device_id_type=MESH,
         )
 
@@ -124,27 +109,47 @@
             device_id_type=MESH,
         )
 
-    for i in range(1, NEAR):
+    for i in (1, 2, 4):
         token_copy(i).start()
+
+    logits = lax.dot_general(
+        router_ref[...], tokens_ref[...], (((1,), (1,)), ((), ())), preferred_element_type=f32
+    )
+    expert_row = lax.broadcasted_iota(jnp.int32, (experts, rows), 0)
+    chosen = jnp.zeros((experts, rows), f32)
+    for k in range(top):
+        chosen = jnp.where(ids_ref[k : k + 1, :] == expert_row, 1.0, chosen)
+    affinity = jnp.where(chosen > 0, 1.0 / (1.0 + jnp.exp(-logits)), 0.0)
+    gates = 2.5 * affinity / jnp.sum(affinity, axis=0, keepdims=True)
+    earlier = lax.broadcasted_iota(jnp.int32, (rows, rows), 0)
+    later = lax.broadcasted_iota(jnp.int32, (rows, rows), 1)
+    upto = jnp.where(earlier <= later, 1.0, 0.0).astype(bf16)
+    ranks = jnp.dot(chosen.astype(bf16), upto, preferred_element_type=f32)
+    route[...] = jnp.concatenate([chosen * ranks, gates], axis=1)
+    routes[0, 0] = route[...]
+    for i in range(1, NEAR):
         route_copy(i).start()
 
     def landed(ref, sem):
         pltpu.make_async_copy(ref, ref, sem).wait()
 
-    def wait_block(m, q):
+    def wait_tokens(m, q):
         landed(gathered.at[m, pl.ds(q * rows, rows)], g_recv.at[m * 2 + q])
+
+    def wait_route(m, q):
         landed(routes.at[m, q], r_recv.at[m * 2 + q])
 
-    def spread(m, base):
-        first_half = lax.broadcasted_iota(jnp.int32, (1, 2 * rows), 1) < rows
-        bands = []
-        for place in range(NEAR):
-            expert = base + served_device(place)
-            row = jnp.where(
-                first_half, routes[m, 0, pl.ds(expert, 1), :], routes[m, 1, pl.ds(expert, 1), :]
-            )
-            bands.append(jnp.broadcast_to(row, (slot_rows, 2 * rows)))
-        return jnp.concatenate(bands, axis=0)
+    def spread(m, gate):
+        half = lax.broadcasted_iota(jnp.int32, (NEAR, 2 * rows), 1) // rows
+
+        def picked(q):
+            table = [routes[m, q, pl.ds(served_device(place), 1), :] for place in range(NEAR)]
+            table = jnp.concatenate(table, axis=0)
+            return table if gate == q else jnp.concatenate([table[:, rows:], table[:, :rows]], axis=1)
+
+        table = jnp.where(half == 0, picked(0), picked(1))
+        table = jnp.broadcast_to(table[:, None, :], (NEAR, slot_rows, 2 * rows))
+        return table.reshape(NEAR * slot_rows, 2 * rows)
 
     def taken(m):
         slot = lax.broadcasted_iota(jnp.int32, (NEAR * slot_rows, 2 * rows), 0) % slot_rows
@@ -178,9 +183,11 @@
     def pack_and_send(m, carry):
         @pl.when(m > 0)
         def _():
-            wait_block(m, 0)
-
-        wait_block(m, 1)
+            wait_tokens(m, 0)
+            wait_route(m, 0)
+            wait_tokens(m, 1)
+
+        wait_route(m, 1)
         pack_chunk(m)
 
         def send(k, carry):
@@ -195,12 +202,22 @@
         ).start()
         return carry
 
+    wait_tokens(0, 1)
+    for i in (3, 5, 6, 7):
+        token_copy(i).start()
+
     lax.fori_loop(0, 4, pack_and_send, 0)
+    for i in range(1, NEAR):
+        token_copy(i).wait_send()
 
     plane = jnp.zeros((experts, 2 * rows), f32)
     for i in range(NEAR):
-        plane = plane + jnp.where(routes[i // 2, i % 2, 0:experts, :] > 0, 0.5, 0.0)
-    tally[...] = plane
+        plane = plane + jnp.where(routes[i // 2, i % 2] > 0, 1.0, 0.0)
+    ones = jnp.where(lax.broadcasted_iota(jnp.int32, (8, 2 * rows), 1) < rows, 1.0, 0.0).astype(bf16)
+    tally[...] = jnp.zeros_like(tally)
+    tally[:, 0:experts] = lax.dot_general(
+        ones, plane.astype(bf16), (((1,), (1,)), ((), ())), preferred_element_type=f32
+    )
 
     def tally_copy(k):
         return pltpu.make_async_remote_copy(
@@ -272,9 +289,56 @@
         ).start()
         return carry
 
-    lax.fori_loop(0, 4, serve, 0)
-
-    group = jnp.zeros((experts, 2 * rows), f32)
+    def sum_copy(m, q):
+        slot = chunk_there(m)
+        return pltpu.make_async_remote_copy(
+            src_ref=gathered.at[m, pl.ds(q * rows, rows)],
+            dst_ref=sums.at[slot * 2 + q],
+            send_sem=p_send.at[m * 2 + q],
+            recv_sem=p_recv.at[slot * 2 + q],
+            device_id=(dp, plane_device(m, q)),
+            device_id_type=MESH,
+        )
+
+    def combine(m, carry):
+        def arrive(place, carry):
+            landed(back.at[m, rows_of(place)], t_recv.at[m * NEAR + place])
+            return carry
+
+        lax.fori_loop(0, NEAR, arrive, 0)
+        weight = jnp.where(taken(m), spread(m, 1), 0.0).T
+        high = weight.astype(bf16)
+        low = (weight - high.astype(f32)).astype(bf16)
+
+        def tile(n, carry):
+            columns = pl.ds(pl.multiple_of(n * 512, 512), 512)
+            block = back[m, :, columns]
+            total = jnp.dot(high, block, preferred_element_type=f32)
+            total = total + jnp.dot(low, block, preferred_element_type=f32)
+            gathered[m, :, columns] = total.astype(bf16)
+            return carry
+
+        lax.fori_loop(0, depth // 512, tile, 0)
+
+        @pl.when(m > 0)
+        def _():
+            sum_copy(m, 0).start()
+
+        sum_copy(m, 1).start()
+        return carry
+
+    def serve_and_combine(m, carry):
+        serve(m, carry)
+
+        @pl.when(m >= 2)
+        def _():
+            combine(m - 2, 0)
+
+        return carry
+
+    lax.fori_loop(0, 4, serve_and_combine, 0)
+
+    group = jnp.zeros((8, 2 * experts), f32)
     for source in range(NEAR):
         landed(tallies.at[source], c_recv.at[source])
         group = group + tallies[source]
@@ -289,51 +353,25 @@
     )
     twin_copy.start()
 
-    def sum_copy(m, q):
-        slot = chunk_there(m)
-        return pltpu.make_async_remote_copy(
-            src_ref=gathered.at[m, pl.ds(q * rows, rows)],
-            dst_ref=sums.at[slot * 2 + q],
-            send_sem=p_send.at[m * 2 + q],
-            recv_sem=p_recv.at[slot * 2 + q],
-            device_id=(dp, plane_device(m, q)),
-            device_id_type=MESH,
-        )
-
-    def combine(m, carry):
-        def arrive(place, carry):
-            landed(back.at[m, rows_of(place)], t_recv.at[m * NEAR + place])
-            return carry
-
-        lax.fori_loop(0, NEAR, arrive, 0)
-        weight = jnp.where(taken(m), spread(m, experts), 0.0).T
-        high = weight.astype(bf16)
-        low = (weight - high.astype(f32)).astype(bf16)
-
-        def tile(n, carry):
-            columns = pl.ds(pl.multiple_of(n * 512, 512), 512)
-            block = back[m, :, columns]
-            total = jnp.dot(high, block, preferred_element_type=f32)
-            total = total + jnp.dot(low, block, preferred_element_type=f32)
-            gathered[m, :, columns] = total.astype(bf16)
-            return carry
-
-        lax.fori_loop(0, depth // 512, tile, 0)
-
-        @pl.when(m > 0)
-        def _():
-            sum_copy(m, 0).start()
-
-        sum_copy(m, 1).start()
-        return carry
-
-    lax.fori_loop(0, 4, combine, 0)
+    lax.fori_loop(2, 4, combine, 0)
 
     twin_copy.wait()
-    pairs = (twin[0] + twin[1]) * (1.0 / 1024.0)
-    load_ref[...] = jnp.sum(
-        jnp.concatenate([pairs, jnp.zeros_like(pairs)], axis=0).T, axis=0, keepdims=True
-    )
+    load_ref[...] = (twin[0, 0:1, 0:experts] + twin[1, 0:1, 0:experts]) * (1.0 / 1024.0)
+
+    for i in range(1, NEAR):
+        route_copy(i).wait_send()
+
+    def sent(k, carry):
+        tally_copy(k).wait_send()
+
+        def sent_chunk(m, carry):
+            hand_out(m, k).wait_send()
+            hand_back(m, k).wait_send()
+            return carry
+
+        return lax.fori_loop(0, 4, sent_chunk, carry)
+
+    lax.fori_loop(1, NEAR, sent, 0)
 
     for i in range(1, NEAR):
         landed(sums.at[i], p_recv.at[i])
@@ -349,21 +387,7 @@
     lax.fori_loop(0, depth // 512, finish, 0)
 
     for i in range(1, NEAR):
-        token_copy(i).wait_send()
-        route_copy(i).wait_send()
         sum_copy(i // 2, i % 2).wait_send()
-
-    def sent(k, carry):
-        tally_copy(k).wait_send()
-
-        def sent_chunk(m, carry):
-            hand_out(m, k).wait_send()
-            hand_back(m, k).wait_send()
-            return carry
-
-        return lax.fori_loop(0, 4, sent_chunk, carry)
-
-    lax.fori_loop(1, NEAR, sent, 0)
 
 
 def local(tokens, expert_ids, router_weight, gate_weight, up_weight, down_weight):
@@ -380,7 +404,7 @@
         functools.partial(moe_kernel, (rows, depth, width, experts, top)),
         out_shape=(
             jax.ShapeDtypeStruct((rows, depth), bf16),
-            jax.ShapeDtypeStruct((1, 2 * experts), f32),
+            jax.ShapeDtypeStruct((1, experts), f32),
         ),
         in_specs=[vmem, vmem, vmem, hbm, hbm, hbm],
         out_specs=(vmem, vmem),
@@ -389,16 +413,16 @@
             pltpu.VMEM((depth, width), bf16),
             pltpu.VMEM((width, depth), bf16),
             pltpu.VMEM((4, 2 * rows, depth), bf16),
-            pltpu.VMEM((4, 2, 2 * experts, 2 * rows), f32),
+            pltpu.VMEM((4, 2, experts, 2 * rows), f32),
             pltpu.VMEM((4, slots, depth), bf16),
             pltpu.VMEM((4, slots, depth), bf16),
             pltpu.VMEM((4, slots, depth), bf16),
             pltpu.VMEM((NEAR, rows, depth), bf16),
             pltpu.VMEM((slots, width), bf16),
-            pltpu.VMEM((2 * experts, 2 * rows), f32),
             pltpu.VMEM((experts, 2 * rows), f32),
-            pltpu.VMEM((NEAR, experts, 2 * rows), f32),
-            pltpu.VMEM((2, experts, 2 * rows), f32),
+            pltpu.VMEM((8, 2 * experts), f32),
+            pltpu.VMEM((NEAR, 8, 2 * experts), f32),
+            pltpu.VMEM((2, 8, 2 * experts), f32),
             dma((3,)),
             dma((NEAR,)), dma((NEAR,)),
             dma((NEAR,)), dma((NEAR,)),
@@ -411,8 +435,8 @@
         compiler_params=pltpu.CompilerParams(
             collective_id=0, has_side_effects=True, vmem_limit_bytes=60 * 1024 * 1024
         ),
-    )(tokens, expert_ids, router_weight, gate_weight, up_weight, down_weight)
-    return mixed, load[0, :experts]
+    )(tokens, expert_ids.T, router_weight.T, gate_weight, up_weight, down_weight)
+    return mixed, load.reshape(experts)
 
 
 def solution(mesh):

time: 185 us -> 164 us (0.89)
  Pallas kernels: 175 us -> 157 us
  local copies, waits for them, and re-layouts: 6.64 us -> 3.01 us
    pallas_call x1, Pallas kernels: 175 us -> 157 us  [local(): pl.pallas_call(functools.partial(moe_kernel, (rows, depth, width, experts...]
    unnamed x3 -> x2, local copies, waits for them, and re-layouts: 5.46 us -> 3.01 us
where the time goes in v1:
time: 164 us; the launch traced here: 161 us
  Pallas kernels  157 us (96%)
  local copies, waits for them, and re-layouts  3.01 us (2%)
    pallas_call x1, Pallas kernels, local(): pl.pallas_call(functools.partial(moe_kernel, (rows, depth, width, experts...  157 us

profile of v1, /device:TPU:1, one launch (start us, length us, event | category | flops | bytes accessed | tf_op | source)
XLA Modules:
  0.0 161.1 jit_solution(6556487858325109212)
XLA Ops:
  0.6 157.4 %shard_map.77 = (bf16[64,3584]{1,0:T(8,128)(2,1)}, f32[1,64]{1,0:T(1,128)}) custom-call(bf16[64,3584]{1,0:T(8,128)(2,1)} %tokens_ref.1, s32[8,64]{1,0:T(8,128)} %bitcast.4, bf16[64,3584]{1,0:T(8,128)(2,1)} %bitcast.3, bf16[1,3584,1024]{2,1,0:T(8,128)(2,1)} %wg_hbm.1, bf16[1,3584,1024]{2,1,0:T(8,128)(2,1)} %wu_hbm.1, bf16[1,1024,3584]{2,1,0:T(8,128)(2,1)} %wd_hbm.1), custom_call_target="tpu_custom_call" | custom-call | tf_op jit(solution)/shard_map/pallas_call | solution.py:403
  158.1 1.8 %copy.10 = bf16[64,3584]{1,0:T(8,128)(2,1)} copy(bf16[64,3584]{1,0:T(8,128)(2,1)} %get-tuple-element.8) | data formatting | bytes 917504
  159.9 1.2 copy.11

commit v2 on v1

--- a/solution.py
+++ b/solution.py
@@ -8,6 +8,7 @@
 from jax.sharding import PartitionSpec as P
 
 MESH = pl.DeviceIdType.MESH
+VIA_PEER = (1, 2)
 CAP = 16
 NEAR = 8
 
@@ -16,7 +17,7 @@
     sizes,
     tokens_ref, ids_ref, router_ref, wg_hbm, wu_hbm, wd_hbm,
     mixed_ref, load_ref,
-    wg, wu, wd, gathered, routes, packed, served, back, sums, hidden, route, tally, tallies, twin,
+    wg, wu, wd, gathered, routes, packed, served, back, sums, so_far, hidden, route, tally, tallies, twin,
     w_sem, g_send, g_recv, r_send, r_recv, d_send, d_recv, t_send, t_recv, p_send, p_recv,
     c_send, c_recv, x_send, x_recv,
 ):
@@ -84,16 +85,24 @@
     gathered[0, 0:rows, :] = tokens_ref[...]
     pl.semaphore_wait(barrier, 3 * (NEAR - 1) + 1)
 
-    def token_copy(i):
-        m, q = i // 2, i % 2
+    def axis_copy(m):
         slot = chunk_there(m)
-        relayed = m > 0 and q == 1
-        return pltpu.make_async_remote_copy(
-            src_ref=gathered.at[0, pl.ds(rows, rows)] if relayed else tokens_ref,
-            dst_ref=gathered.at[slot, pl.ds(q * rows, rows)],
-            send_sem=g_send.at[i],
-            recv_sem=g_recv.at[slot * 2 + q],
-            device_id=(dp, plane_device(m, 0 if relayed else q)),
+        return pltpu.make_async_remote_copy(
+            src_ref=tokens_ref,
+            dst_ref=gathered.at[slot, pl.ds(0, rows)],
+            send_sem=g_send.at[m * 2],
+            recv_sem=g_recv.at[slot * 2],
+            device_id=(dp, plane_device(m, 0)),
+            device_id_type=MESH,
+        )
+
+    def peer_copy(m):
+        return pltpu.make_async_remote_copy(
+            src_ref=gathered.at[m, pl.ds(0, rows)],
+            dst_ref=gathered.at[m, pl.ds(rows, rows)],
+            send_sem=g_send.at[m * 2 + 1],
+            recv_sem=g_recv.at[m * 2 + 1],
+            device_id=(dp, plane_device(0, 1)),
             device_id_type=MESH,
         )
 
@@ -109,8 +118,9 @@
             device_id_type=MESH,
         )
 
-    for i in (1, 2, 4):
-        token_copy(i).start()
+    peer_copy(0).start()
+    for m in range(1, 4):
+        axis_copy(m).start()
 
     logits = lax.dot_general(
         router_ref[...], tokens_ref[...], (((1,), (1,)), ((), ())), preferred_element_type=f32
@@ -180,12 +190,17 @@
             device_id_type=MESH,
         )
 
-    def pack_and_send(m, carry):
+    def pack_and_send(m):
+        wait_tokens(m, 1)
+
+        @pl.when(m < 3)
+        def _():
+            wait_tokens(m + 1, 0)
+            peer_copy(m + 1).start()
+
         @pl.when(m > 0)
         def _():
-            wait_tokens(m, 0)
             wait_route(m, 0)
-            wait_tokens(m, 1)
 
         wait_route(m, 1)
         pack_chunk(m)
@@ -200,15 +215,139 @@
             served.at[m, rows_of(my_source)],
             d_recv.at[m * NEAR + my_source],
         ).start()
-        return carry
-
-    wait_tokens(0, 1)
-    for i in (3, 5, 6, 7):
-        token_copy(i).start()
-
-    lax.fori_loop(0, 4, pack_and_send, 0)
-    for i in range(1, NEAR):
-        token_copy(i).wait_send()
+
+
+    def hand_back(m, k):
+        source = (my_source + k) % NEAR
+        place = place_there(source)
+        return pltpu.make_async_remote_copy(
+            src_ref=served.at[m, rows_of(source)],
+            dst_ref=back.at[m, rows_of(place)],
+            send_sem=t_send.at[m * NEAR + k],
+            recv_sem=t_recv.at[m * NEAR + place],
+            device_id=(dp, source_device(source)),
+            device_id_type=MESH,
+        )
+
+    def serve(m, carry):
+        def arrive(source, carry):
+            landed(served.at[m, rows_of(source)], d_recv.at[m * NEAR + source])
+            return carry
+
+        lax.fori_loop(0, NEAR, arrive, 0)
+
+        def into_hidden(n, carry):
+            columns = pl.ds(pl.multiple_of(n * 256, 256), 256)
+            gate_part = jnp.dot(served[m], wg[:, columns], preferred_element_type=f32)
+            up_part = jnp.dot(served[m], wu[:, columns], preferred_element_type=f32)
+            act = gate_part / (1.0 + jnp.exp(-gate_part)) * up_part
+            hidden[:, columns] = act.astype(bf16)
+            return carry
+
+        lax.fori_loop(0, width // 256, into_hidden, 0)
+
+        def out_of_hidden(n, carry):
+            columns = pl.ds(pl.multiple_of(n * 512, 512), 512)
+            served[m, :, columns] = jnp.dot(
+                hidden[...], wd[:, columns], preferred_element_type=f32
+            ).astype(bf16)
+            return carry
+
+        lax.fori_loop(0, depth // 512, out_of_hidden, 0)
+
+        def send(k, carry):
+            hand_back(m, k).start()
+            return carry
+
+        lax.fori_loop(1, NEAR, send, 0)
+        pltpu.make_async_copy(
+            served.at[m, rows_of(my_source)],
+            back.at[m, rows_of(my_place)],
+            t_recv.at[m * NEAR + my_place],
+        ).start()
+        return carry
+
+    def sum_copy(m, q):
+        slot = chunk_there(m)
+        return pltpu.make_async_remote_copy(
+            src_ref=gathered.at[m, pl.ds(q * rows, rows)],
+            dst_ref=sums.at[slot * 2 + q],
+            send_sem=p_send.at[m * 2 + q],
+            recv_sem=p_recv.at[slot * 2 + q],
+            device_id=(dp, plane_device(m, q)),
+            device_id_type=MESH,
+        )
+
+    def peer_sum_copy(m):
+        return pltpu.make_async_remote_copy(
+            src_ref=gathered.at[m, pl.ds(rows, rows)],
+            dst_ref=sums.at[m * 2 + 1],
+            send_sem=p_send.at[m * 2 + 1],
+            recv_sem=p_recv.at[m * 2 + 1],
+            device_id=(dp, plane_device(0, 1)),
+            device_id_type=MESH,
+        )
+
+    def combine(m):
+        peer_copy(m).wait_send()
+        def arrive(place, carry):
+            landed(back.at[m, rows_of(place)], t_recv.at[m * NEAR + place])
+            return carry
+
+        lax.fori_loop(0, NEAR, arrive, 0)
+        weight = jnp.where(taken(m), spread(m, 1), 0.0).T
+        high = weight.astype(bf16)
+        low = (weight - high.astype(f32)).astype(bf16)
+
+        def tile(n, carry):
+            columns = pl.ds(pl.multiple_of(n * 512, 512), 512)
+            block = back[m, :, columns]
+            total = jnp.dot(high, block, preferred_element_type=f32)
+            total = total + jnp.dot(low, block, preferred_element_type=f32)
+            gathered[m, :, columns] = total.astype(bf16)
+            return carry
+
+        lax.fori_loop(0, depth // 512, tile, 0)
+
+        if m in VIA_PEER:
+            peer_sum_copy(m).start()
+        else:
+            if m > 0:
+                sum_copy(m, 0).start()
+            sum_copy(m, 1).start()
+
+    def pass_on(m):
+        landed(sums.at[m * 2 + 1], p_recv.at[m * 2 + 1])
+
+        def tile(n, carry):
+            columns = pl.ds(pl.multiple_of(n * 512, 512), 512)
+            both = gathered[m, 0:rows, columns].astype(f32) + sums[m * 2 + 1, :, columns].astype(f32)
+            gathered[m, 0:rows, columns] = both.astype(bf16)
+            return carry
+
+        lax.fori_loop(0, depth // 512, tile, 0)
+        sum_copy(m, 0).start()
+
+    def pack_first(m, carry):
+        pack_and_send(m)
+        return carry
+
+    lax.fori_loop(0, 2, pack_first, 0)
+    for copy in weights:
+        copy.wait()
+
+    def serve_and_pack(m, carry):
+        serve(m, carry)
+        pack_and_send(m + 2)
+        return carry
+
+    lax.fori_loop(0, 2, serve_and_pack, 0)
+    combine(0)
+    serve(2, 0)
+    combine(1)
+    serve(3, 0)
+    pass_on(1)
+    combine(2)
 
     plane = jnp.zeros((experts, 2 * rows), f32)
     for i in range(NEAR):
@@ -236,107 +375,6 @@
     lax.fori_loop(1, NEAR, send_tally, 0)
     pltpu.make_async_copy(tally, tallies.at[my_source], c_recv.at[my_source]).start()
 
-    for copy in weights:
-        copy.wait()
-
-    def hand_back(m, k):
-        source = (my_source + k) % NEAR
-        place = place_there(source)
-        return pltpu.make_async_remote_copy(
-            src_ref=served.at[m, rows_of(source)],
-            dst_ref=back.at[m, rows_of(place)],
-            send_sem=t_send.at[m * NEAR + k],
-            recv_sem=t_recv.at[m * NEAR + place],
-            device_id=(dp, source_device(source)),
-            device_id_type=MESH,
-        )
-
-    def serve(m, carry):
-        def arrive(source, carry):
-            landed(served.at[m, rows_of(source)], d_recv.at[m * NEAR + source])
-            return carry
-
-        lax.fori_loop(0, NEAR, arrive, 0)
-
-        def into_hidden(n, carry):
-            columns = pl.ds(pl.multiple_of(n * 256, 256), 256)
-            gate_part = jnp.dot(served[m], wg[:, columns], preferred_element_type=f32)
-            up_part = jnp.dot(served[m], wu[:, columns], preferred_element_type=f32)
-            act = gate_part / (1.0 + jnp.exp(-gate_part)) * up_part
-            hidden[:, columns] = act.astype(bf16)
-            return carry
-
-        lax.fori_loop(0, width // 256, into_hidden, 0)
-
-        def out_of_hidden(n, carry):
-            columns = pl.ds(pl.multiple_of(n * 512, 512), 512)
-            served[m, :, columns] = jnp.dot(
-                hidden[...], wd[:, columns], preferred_element_type=f32
-            ).astype(bf16)
-            return carry
-
-        lax.fori_loop(0, depth // 512, out_of_hidden, 0)
-
-        def send(k, carry):
-            hand_back(m, k).start()
-            return carry
-
-        lax.fori_loop(1, NEAR, send, 0)
-        pltpu.make_async_copy(
-            served.at[m, rows_of(my_source)],
-            back.at[m, rows_of(my_place)],
-            t_recv.at[m * NEAR + my_place],
-        ).start()
-        return carry
-
-    def sum_copy(m, q):
-        slot = chunk_there(m)
-        return pltpu.make_async_remote_copy(
-            src_ref=gathered.at[m, pl.ds(q * rows, rows)],
-            dst_ref=sums.at[slot * 2 + q],
-            send_sem=p_send.at[m * 2 + q],
-            recv_sem=p_recv.at[slot * 2 + q],
-            device_id=(dp, plane_device(m, q)),
-            device_id_type=MESH,
-        )
-
-    def combine(m, carry):
-        def arrive(place, carry):
-            landed(back.at[m, rows_of(place)], t_recv.at[m * NEAR + place])
-            return carry
-
-        lax.fori_loop(0, NEAR, arrive, 0)
-        weight = jnp.where(taken(m), spread(m, 1), 0.0).T
-        high = weight.astype(bf16)
-        low = (weight - high.astype(f32)).astype(bf16)
-
-        def tile(n, carry):
-            columns = pl.ds(pl.multiple_of(n * 512, 512), 512)
-            block = back[m, :, columns]
-            total = jnp.dot(high, block, preferred_element_type=f32)
-            total = total + jnp.dot(low, block, preferred_element_type=f32)
-            gathered[m, :, columns] = total.astype(bf16)
-            return carry
-
-        lax.fori_loop(0, depth // 512, tile, 0)
-
-        @pl.when(m > 0)
-        def _():
-            sum_copy(m, 0).start()
-
-        sum_copy(m, 1).start()
-        return carry
-
-    def serve_and_combine(m, carry):
-        serve(m, carry)
-
-        @pl.when(m >= 2)
-        def _():
-            combine(m - 2, 0)
-
-        return carry
-
-    lax.fori_loop(0, 4, serve_and_combine, 0)
 
     group = jnp.zeros((8, 2 * experts), f32)
     for source in range(NEAR):
@@ -353,11 +391,16 @@
     )
     twin_copy.start()
 
-    lax.fori_loop(2, 4, combine, 0)
+    pass_on(2)
+    combine(3)
+    if 3 in VIA_PEER:
+        pass_on(3)
 
     twin_copy.wait()
     load_ref[...] = (twin[0, 0:1, 0:experts] + twin[1, 0:1, 0:experts]) * (1.0 / 1024.0)
 
+    for m in range(1, 4):
+        axis_copy(m).wait_send()
     for i in range(1, NEAR):
         route_copy(i).wait_send()
 
@@ -373,21 +416,35 @@
 
     lax.fori_loop(1, NEAR, sent, 0)
 
-    for i in range(1, NEAR):
+    early, late = [1, 2, 4], [6] if 3 in VIA_PEER else [6, 7]
+    for i in early:
+        landed(sums.at[i], p_recv.at[i])
+
+    def gather_early(n, carry):
+        columns = pl.ds(pl.multiple_of(n * 512, 512), 512)
+        total = gathered[0, 0:rows, columns].astype(f32)
+        for i in early:
+            total = total + sums[i, :, columns].astype(f32)
+        so_far[:, columns] = total
+        return carry
+
+    lax.fori_loop(0, depth // 512, gather_early, 0)
+    for i in late:
         landed(sums.at[i], p_recv.at[i])
 
     def finish(n, carry):
         columns = pl.ds(pl.multiple_of(n * 512, 512), 512)
-        total = gathered[0, 0:rows, columns].astype(f32)
-        for i in range(1, NEAR):
+        total = so_far[:, columns]
+        for i in late:
             total = total + sums[i, :, columns].astype(f32)
         mixed_ref[:, columns] = total.astype(bf16)
         return carry
 
     lax.fori_loop(0, depth // 512, finish, 0)
-
-    for i in range(1, NEAR):
-        sum_copy(i // 2, i % 2).wait_send()
+    sum_copy(0, 1).wait_send()
+    for m in range(1, 4):
+        sum_copy(m, 0).wait_send()
+        (peer_sum_copy(m) if m in VIA_PEER else sum_copy(m, 1)).wait_send()
 
 
 def local(tokens, expert_ids, router_weight, gate_weight, up_weight, down_weight):
@@ -418,6 +475,7 @@
             pltpu.VMEM((4, slots, depth), bf16),
             pltpu.VMEM((4, slots, depth), bf16),
             pltpu.VMEM((NEAR, rows, depth), bf16),
+            pltpu.VMEM((rows, depth), f32),
             pltpu.VMEM((slots, width), bf16),
             pltpu.VMEM((experts, 2 * rows), f32),
             pltpu.VMEM((8, 2 * experts), f32),

time: 164 us -> 138 us (0.84); the launches traced: 161 us -> 138 us
  Pallas kernels: 157 us -> 135 us
    pallas_call x1, Pallas kernels: 157 us -> 135 us  [local(): pl.pallas_call(functools.partial(moe_kernel, (rows, depth, width, experts...]
where the time goes in v2:
time: 138 us
  Pallas kernels  135 us (98%)
  local copies, waits for them, and re-layouts  3.01 us (2%)
    pallas_call x1, Pallas kernels, local(): pl.pallas_call(functools.partial(moe_kernel, (rows, depth, width, experts...  135 us
    unnamed x2, local copies, waits for them, and re-layouts  3.01 us

profile of v2, /device:TPU:1, one launch (start us, length us, event | category | flops | bytes accessed | tf_op | source)
XLA Modules:
  0.0 138.2 jit_solution(14837352088141493374)
XLA Ops:
  0.6 134.5 %shard_map.77 = (bf16[64,3584]{1,0:T(8,128)(2,1)}, f32[1,64]{1,0:T(1,128)}) custom-call(bf16[64,3584]{1,0:T(8,128)(2,1)} %tokens_ref.1, s32[8,64]{1,0:T(8,128)} %bitcast.4, bf16[64,3584]{1,0:T(8,128)(2,1)} %bitcast.3, bf16[1,3584,1024]{2,1,0:T(8,128)(2,1)} %wg_hbm.1, bf16[1,3584,1024]{2,1,0:T(8,128)(2,1)} %wu_hbm.1, bf16[1,1024,3584]{2,1,0:T(8,128)(2,1)} %wd_hbm.1), custom_call_target="tpu_custom_call" | custom-call | tf_op jit(solution)/shard_map/pallas_call | solution.py:460
  135.2 1.8 %copy.10 = bf16[64,3584]{1,0:T(8,128)(2,1)} copy(bf16[64,3584]{1,0:T(8,128)(2,1)} %get-tuple-element.8) | data formatting | bytes 917504
  137.0 1.2 copy.11

commit v3 on v2

--- a/solution.py
+++ b/solution.py
@@ -8,7 +8,9 @@
 from jax.sharding import PartitionSpec as P
 
 MESH = pl.DeviceIdType.MESH
+CHUNKS = (((1, 0), (2, 0)), ((0, 1), (1, 1)), ((3, 0), (2, 1)), ((0, 0), (3, 1)))
 VIA_PEER = (1, 2)
+FORWARD = {(1, 0): 1, (0, 1): 2, (1, 1): 3}
 CAP = 16
 NEAR = 8
 
@@ -149,73 +151,75 @@
     def wait_route(m, q):
         landed(routes.at[m, q], r_recv.at[m * 2 + q])
 
-    def spread(m, gate):
-        half = lax.broadcasted_iota(jnp.int32, (NEAR, 2 * rows), 1) // rows
-
-        def picked(q):
-            table = [routes[m, q, pl.ds(served_device(place), 1), :] for place in range(NEAR)]
-            table = jnp.concatenate(table, axis=0)
-            return table if gate == q else jnp.concatenate([table[:, rows:], table[:, :rows]], axis=1)
-
-        table = jnp.where(half == 0, picked(0), picked(1))
-        table = jnp.broadcast_to(table[:, None, :], (NEAR, slot_rows, 2 * rows))
-        return table.reshape(NEAR * slot_rows, 2 * rows)
-
-    def taken(m):
+    def table(m, q):
+        picked = [routes[m, q, pl.ds(served_device(place), 1), :] for place in range(NEAR)]
+        return jnp.concatenate(picked, axis=0)
+
+    def per_slot(values, count):
+        values = jnp.broadcast_to(values[:, None, :], (NEAR, count, values.shape[1]))
+        return values.reshape(NEAR * count, values.shape[2])
+
+    def pack_block(j, w):
+        m, q = CHUNKS[j][w]
+        codes = per_slot(table(m, q)[:, :rows], CAP)
+        slot = lax.broadcasted_iota(jnp.int32, (NEAR * CAP, rows), 0) % CAP
+        select = jnp.where(codes == (slot + 1).astype(f32), 1.0, 0.0).astype(bf16)
+
+        def tile(n, carry):
+            columns = pl.ds(pl.multiple_of(n * 512, 512), 512)
+            block = gathered[m, q * rows : (q + 1) * rows, columns]
+            packed[j, w, :, columns] = jnp.dot(select, block, preferred_element_type=f32).astype(bf16)
+            return carry
+
+        lax.fori_loop(0, depth // 512, tile, 0)
+
+    def weights_of(j):
+        (m, q), (far_m, far_q) = CHUNKS[j]
+        near, far = table(m, q), table(far_m, far_q)
+        half = lax.broadcasted_iota(jnp.int32, (NEAR, 2 * rows), 1) < rows
+        swap = lambda t: jnp.concatenate([t[:, rows:], t[:, :rows]], axis=1)
+        codes = per_slot(jnp.where(half, near, swap(far)), slot_rows)
+        gates = per_slot(jnp.where(half, swap(near), far), slot_rows)
         slot = lax.broadcasted_iota(jnp.int32, (NEAR * slot_rows, 2 * rows), 0) % slot_rows
         block = lax.broadcasted_iota(jnp.int32, (NEAR * slot_rows, 2 * rows), 1) // rows
         wanted = jnp.where(slot // CAP == block, slot % CAP + 1, -1).astype(f32)
-        return spread(m, 0) == wanted
-
-    def pack_chunk(m):
-        select = jnp.where(taken(m), 1.0, 0.0).astype(bf16)
-
-        def tile(n, carry):
-            columns = pl.ds(pl.multiple_of(n * 512, 512), 512)
-            packed[m, :, columns] = jnp.dot(
-                select, gathered[m, :, columns], preferred_element_type=f32
-            ).astype(bf16)
-            return carry
-
-        lax.fori_loop(0, depth // 512, tile, 0)
-
-    def hand_out(m, k):
+        return jnp.where(codes == wanted, gates, 0.0)
+
+    def hand_out(i, k):
         place = (my_place + k) % NEAR
-        return pltpu.make_async_remote_copy(
-            src_ref=packed.at[m, rows_of(place)],
-            dst_ref=served.at[m, rows_of(my_source)],
-            send_sem=d_send.at[m * NEAR + k],
-            recv_sem=d_recv.at[m * NEAR + my_source],
+        j, w = i // 2, i % 2
+        return pltpu.make_async_remote_copy(
+            src_ref=packed.at[j, w, pl.ds(pl.multiple_of(place * CAP, CAP), CAP)],
+            dst_ref=served.at[j, half_rows_of(my_source, w)],
+            send_sem=d_send.at[i * NEAR + k],
+            recv_sem=d_recv.at[i * NEAR + my_source],
             device_id=(dp, served_device(place)),
             device_id_type=MESH,
         )
 
-    def pack_and_send(m):
-        wait_tokens(m, 1)
-
-        @pl.when(m < 3)
-        def _():
-            wait_tokens(m + 1, 0)
-            peer_copy(m + 1).start()
-
-        @pl.when(m > 0)
-        def _():
-            wait_route(m, 0)
-
-        wait_route(m, 1)
-        pack_chunk(m)
+    def half_rows_of(index, w):
+        return pl.ds(pl.multiple_of(index * slot_rows + w * CAP, CAP), CAP)
+
+    def pack_and_send(j, w):
+        m, q = CHUNKS[j][w]
+        if (m, q) != (0, 0):
+            wait_tokens(m, q)
+            wait_route(m, q)
+        if (m, q) in FORWARD:
+            peer_copy(FORWARD[m, q]).start()
+        pack_block(j, w)
+        i = j * 2 + w
 
         def send(k, carry):
-            hand_out(m, k).start()
+            hand_out(i, k).start()
             return carry
 
         lax.fori_loop(1, NEAR, send, 0)
         pltpu.make_async_copy(
-            packed.at[m, rows_of(my_place)],
-            served.at[m, rows_of(my_source)],
-            d_recv.at[m * NEAR + my_source],
+            packed.at[j, w, pl.ds(pl.multiple_of(my_place * CAP, CAP), CAP)],
+            served.at[j, half_rows_of(my_source, w)],
+            d_recv.at[i * NEAR + my_source],
         ).start()
-
 
     def hand_back(m, k):
         source = (my_source + k) % NEAR
@@ -231,7 +235,8 @@
 
     def serve(m, carry):
         def arrive(source, carry):
-            landed(served.at[m, rows_of(source)], d_recv.at[m * NEAR + source])
+            landed(served.at[m, half_rows_of(source, 0)], d_recv.at[m * 2 * NEAR + source])
+            landed(served.at[m, half_rows_of(source, 1)], d_recv.at[(m * 2 + 1) * NEAR + source])
             return carry
 
         lax.fori_loop(0, NEAR, arrive, 0)
@@ -288,33 +293,37 @@
             device_id_type=MESH,
         )
 
-    def combine(m):
-        peer_copy(m).wait_send()
+    def combine(j):
+        (m, q), (far_m, far_q) = CHUNKS[j]
+
         def arrive(place, carry):
-            landed(back.at[m, rows_of(place)], t_recv.at[m * NEAR + place])
+            landed(back.at[j, rows_of(place)], t_recv.at[j * NEAR + place])
             return carry
 
         lax.fori_loop(0, NEAR, arrive, 0)
-        weight = jnp.where(taken(m), spread(m, 1), 0.0).T
+        for place, other in CHUNKS[j]:
+            if other == 0:
+                peer_copy(place).wait_send()
+        weight = weights_of(j).T
         high = weight.astype(bf16)
         low = (weight - high.astype(f32)).astype(bf16)
 
         def tile(n, carry):
             columns = pl.ds(pl.multiple_of(n * 512, 512), 512)
-            block = back[m, :, columns]
+            block = back[j, :, columns]
             total = jnp.dot(high, block, preferred_element_type=f32)
-            total = total + jnp.dot(low, block, preferred_element_type=f32)
-            gathered[m, :, columns] = total.astype(bf16)
+            total = (total + jnp.dot(low, block, preferred_element_type=f32)).astype(bf16)
+            gathered[m, q * rows : (q + 1) * rows, columns] = total[:rows]
+            gathered[far_m, far_q * rows : (far_q + 1) * rows, columns] = total[rows:]
             return carry
 
         lax.fori_loop(0, depth // 512, tile, 0)
-
-        if m in VIA_PEER:
-            peer_sum_copy(m).start()
-        else:
-            if m > 0:
-                sum_copy(m, 0).start()
-            sum_copy(m, 1).start()
+        for place, other in CHUNKS[j]:
+            if place in VIA_PEER:
+                if other == 1:
+                    peer_sum_copy(place).start()
+            elif (place, other) != (0, 0):
+                sum_copy(place, other).start()
 
     def pass_on(m):
         landed(sums.at[m * 2 + 1], p_recv.at[m * 2 + 1])
@@ -328,26 +337,23 @@
         lax.fori_loop(0, depth // 512, tile, 0)
         sum_copy(m, 0).start()
 
-    def pack_first(m, carry):
-        pack_and_send(m)
-        return carry
-
-    lax.fori_loop(0, 2, pack_first, 0)
+    def serve_chunk(m):
+        lax.fori_loop(m, m + 1, serve, 0)
+
+    for j, w in ((3, 0), (0, 0), (0, 1), (2, 0), (1, 0), (1, 1)):
+        pack_and_send(j, w)
     for copy in weights:
         copy.wait()
-
-    def serve_and_pack(m, carry):
-        serve(m, carry)
-        pack_and_send(m + 2)
-        return carry
-
-    lax.fori_loop(0, 2, serve_and_pack, 0)
+    serve_chunk(0)
+    pack_and_send(2, 1)
+    serve_chunk(1)
+    pack_and_send(3, 1)
     combine(0)
-    serve(2, 0)
+    serve_chunk(2)
     combine(1)
-    serve(3, 0)
+    serve_chunk(3)
+    combine(2)
     pass_on(1)
-    combine(2)
 
     plane = jnp.zeros((experts, 2 * rows), f32)
     for i in range(NEAR):
@@ -391,10 +397,8 @@
     )
     twin_copy.start()
 
+    combine(3)
     pass_on(2)
-    combine(3)
-    if 3 in VIA_PEER:
-        pass_on(3)
 
     twin_copy.wait()
     load_ref[...] = (twin[0, 0:1, 0:experts] + twin[1, 0:1, 0:experts]) * (1.0 / 1024.0)
@@ -408,7 +412,8 @@
         tally_copy(k).wait_send()
 
         def sent_chunk(m, carry):
-            hand_out(m, k).wait_send()
+            hand_out(m * 2, k).wait_send()
+            hand_out(m * 2 + 1, k).wait_send()
             hand_back(m, k).wait_send()
             return carry
 
@@ -416,7 +421,7 @@
 
     lax.fori_loop(1, NEAR, sent, 0)
 
-    early, late = [1, 2, 4], [6] if 3 in VIA_PEER else [6, 7]
+    early, late = [1, 4, 6], [2, 7]
     for i in early:
         landed(sums.at[i], p_recv.at[i])
 
@@ -471,7 +476,7 @@
             pltpu.VMEM((width, depth), bf16),
             pltpu.VMEM((4, 2 * rows, depth), bf16),
             pltpu.VMEM((4, 2, experts, 2 * rows), f32),
-            pltpu.VMEM((4, slots, depth), bf16),
+            pltpu.VMEM((4, 2, NEAR * CAP, depth), bf16),
             pltpu.VMEM((4, slots, depth), bf16),
             pltpu.VMEM((4, slots, depth), bf16),
             pltpu.VMEM((NEAR, rows, depth), bf16),
@@ -484,7 +489,7 @@
             dma((3,)),
             dma((NEAR,)), dma((NEAR,)),
             dma((NEAR,)), dma((NEAR,)),
-            dma((4 * NEAR,)), dma((4 * NEAR,)),
+            dma((8 * NEAR,)), dma((8 * NEAR,)),
             dma((4 * NEAR,)), dma((4 * NEAR,)),
             dma((NEAR,)), dma((NEAR,)),
             dma((NEAR,)), dma((NEAR,)),

time: 138 us -> 136 us (0.986)
  the two profiles are of different devices: /device:TPU:1 before, /device:TPU:69 now
where the time goes in v3:
time: 136 us
  Pallas kernels  132 us (97%)
  local copies, waits for them, and re-layouts  3.01 us (2%)
    pallas_call x1, Pallas kernels, local(): pl.pallas_call(functools.partial(moe_kernel, (rows, depth, width, experts...  132 us
    unnamed x2, local copies, waits for them, and re-layouts  3.01 us

profile of v3, /device:TPU:69, one launch (start us, length us, event | category | flops | bytes accessed | tf_op | source)
XLA Modules:
  0.0 136.0 jit_solution(15977594914334340058)
XLA Ops:
  0.6 132.4 %shard_map.77 = (bf16[64,3584]{1,0:T(8,128)(2,1)}, f32[1,64]{1,0:T(1,128)}) custom-call(bf16[64,3584]{1,0:T(8,128)(2,1)} %tokens_ref.1, s32[8,64]{1,0:T(8,128)} %bitcast.4, bf16[64,3584]{1,0:T(8,128)(2,1)} %bitcast.3, bf16[1,3584,1024]{2,1,0:T(8,128)(2,1)} %wg_hbm.1, bf16[1,3584,1024]{2,1,0:T(8,128)(2,1)} %wu_hbm.1, bf16[1,1024,3584]{2,1,0:T(8,128)(2,1)} %wd_hbm.1), custom_call_target="tpu_custom_call" | custom-call | tf_op jit(solution)/shard_map/pallas_call | solution.py:465
  133.0 1.8 %copy.10 = bf16[64,3584]{1,0:T(8,128)(2,1)} copy(bf16[64,3584]{1,0:T(8,128)(2,1)} %get-tuple-element.8) | data formatting | bytes 917504
  134.8 1.2 copy.11

commit v4 on v3

--- a/solution.py
+++ b/solution.py
@@ -11,6 +11,7 @@
 CHUNKS = (((1, 0), (2, 0)), ((0, 1), (1, 1)), ((3, 0), (2, 1)), ((0, 0), (3, 1)))
 VIA_PEER = (1, 2)
 FORWARD = {(1, 0): 1, (0, 1): 2, (1, 1): 3}
+PARTS = ((0, 4), (4, 7))
 CAP = 16
 NEAR = 8
 
@@ -21,7 +22,7 @@
     mixed_ref, load_ref,
     wg, wu, wd, gathered, routes, packed, served, back, sums, so_far, hidden, route, tally, tallies, twin,
     w_sem, g_send, g_recv, r_send, r_recv, d_send, d_recv, t_send, t_recv, p_send, p_recv,
-    c_send, c_recv, x_send, x_recv,
+    c_send, c_recv, x_send, x_recv, l_send, l_recv,
 ):
     rows, depth, width, experts, top = sizes
     f32, bf16 = jnp.float32, jnp.bfloat16
@@ -221,14 +222,18 @@
             d_recv.at[i * NEAR + my_source],
         ).start()
 
-    def hand_back(m, k):
+    def part_of(part):
+        first, last = PARTS[part]
+        return pl.ds(first * 512, (last - first) * 512)
+
+    def hand_back(m, k, part):
         source = (my_source + k) % NEAR
         place = place_there(source)
         return pltpu.make_async_remote_copy(
-            src_ref=served.at[m, rows_of(source)],
-            dst_ref=back.at[m, rows_of(place)],
-            send_sem=t_send.at[m * NEAR + k],
-            recv_sem=t_recv.at[m * NEAR + place],
+            src_ref=served.at[m, rows_of(source), part_of(part)],
+            dst_ref=back.at[m, rows_of(place), part_of(part)],
+            send_sem=t_send.at[(m * 2 + part) * NEAR + k],
+            recv_sem=t_recv.at[(m * 2 + part) * NEAR + place],
             device_id=(dp, source_device(source)),
             device_id_type=MESH,
         )
@@ -258,18 +263,19 @@
             ).astype(bf16)
             return carry
 
-        lax.fori_loop(0, depth // 512, out_of_hidden, 0)
-
-        def send(k, carry):
-            hand_back(m, k).start()
-            return carry
-
-        lax.fori_loop(1, NEAR, send, 0)
-        pltpu.make_async_copy(
-            served.at[m, rows_of(my_source)],
-            back.at[m, rows_of(my_place)],
-            t_recv.at[m * NEAR + my_place],
-        ).start()
+        for part, (first, last) in enumerate(PARTS):
+            lax.fori_loop(first, last, out_of_hidden, 0)
+
+            def send(k, carry, part=part):
+                hand_back(m, k, part).start()
+                return carry
+
+            lax.fori_loop(1, NEAR, send, 0)
+            pltpu.make_async_copy(
+                served.at[m, rows_of(my_source), part_of(part)],
+                back.at[m, rows_of(my_place), part_of(part)],
+                t_recv.at[(m * 2 + part) * NEAR + my_place],
+            ).start()
         return carry
 
     def sum_copy(m, q):
@@ -293,14 +299,29 @@
             device_id_type=MESH,
         )
 
+    def last_copy(part):
+        return pltpu.make_async_remote_copy(
+            src_ref=gathered.at[3, pl.ds(rows, rows), part_of(part)],
+            dst_ref=sums.at[7, pl.ds(0, rows), part_of(part)],
+            send_sem=l_send.at[part],
+            recv_sem=l_recv.at[part],
+            device_id=(dp, plane_device(3, 1)),
+            device_id_type=MESH,
+        )
+
     def combine(j):
         (m, q), (far_m, far_q) = CHUNKS[j]
 
-        def arrive(place, carry):
-            landed(back.at[j, rows_of(place)], t_recv.at[j * NEAR + place])
-            return carry
-
-        lax.fori_loop(0, NEAR, arrive, 0)
+        def arrive(part):
+            def one(place, carry):
+                landed(
+                    back.at[j, rows_of(place), part_of(part)],
+                    t_recv.at[(j * 2 + part) * NEAR + place],
+                )
+                return carry
+
+            lax.fori_loop(0, NEAR, one, 0)
+
         for place, other in CHUNKS[j]:
             if other == 0:
                 peer_copy(place).wait_send()
@@ -317,12 +338,16 @@
             gathered[far_m, far_q * rows : (far_q + 1) * rows, columns] = total[rows:]
             return carry
 
-        lax.fori_loop(0, depth // 512, tile, 0)
+        for part, (first, last) in enumerate(PARTS):
+            arrive(part)
+            lax.fori_loop(first, last, tile, 0)
+            if j == 3:
+                last_copy(part).start()
         for place, other in CHUNKS[j]:
             if place in VIA_PEER:
                 if other == 1:
                     peer_sum_copy(place).start()
-            elif (place, other) != (0, 0):
+            elif (place, other) not in ((0, 0), (3, 1)):
                 sum_copy(place, other).start()
 
     def pass_on(m):
@@ -414,7 +439,8 @@
         def sent_chunk(m, carry):
             hand_out(m * 2, k).wait_send()
             hand_out(m * 2 + 1, k).wait_send()
-            hand_back(m, k).wait_send()
+            hand_back(m, k, 0).wait_send()
+            hand_back(m, k, 1).wait_send()
             return carry
 
         return lax.fori_loop(0, 4, sent_chunk, carry)
@@ -434,8 +460,9 @@
         return carry
 
     lax.fori_loop(0, depth // 512, gather_early, 0)
-    for i in late:
-        landed(sums.at[i], p_recv.at[i])
+    landed(sums.at[2], p_recv.at[2])
+    for part in range(2):
+        landed(sums.at[7, pl.ds(0, rows), part_of(part)], l_recv.at[part])
 
     def finish(n, carry):
         columns = pl.ds(pl.multiple_of(n * 512, 512), 512)
@@ -449,7 +476,11 @@
     sum_copy(0, 1).wait_send()
     for m in range(1, 4):
         sum_copy(m, 0).wait_send()
-        (peer_sum_copy(m) if m in VIA_PEER else sum_copy(m, 1)).wait_send()
+        if m in VIA_PEER:
+            peer_sum_copy(m).wait_send()
+        else:
+            last_copy(0).wait_send()
+            last_copy(1).wait_send()
 
 
 def local(tokens, expert_ids, router_weight, gate_weight, up_weight, down_weight):
@@ -490,10 +521,11 @@
             dma((NEAR,)), dma((NEAR,)),
             dma((NEAR,)), dma((NEAR,)),
             dma((8 * NEAR,)), dma((8 * NEAR,)),
-            dma((4 * NEAR,)), dma((4 * NEAR,)),
+            dma((8 * NEAR,)), dma((8 * NEAR,)),
             dma((NEAR,)), dma((NEAR,)),
             dma((NEAR,)), dma((NEAR,)),
             dma, dma,
+            dma((2,)), dma((2,)),
         ],
         compiler_params=pltpu.CompilerParams(
             collective_id=0, has_side_effects=True, vmem_limit_bytes=60 * 1024 * 1024

time: 136 us -> 136 us (level)
  the two profiles are of different devices: /device:TPU:69 before, /device:TPU:91 now
where the time goes in v4:
time: 136 us
  Pallas kernels  132 us (97%)
  local copies, waits for them, and re-layouts  3.01 us (2%)
    pallas_call x1, Pallas kernels, local(): pl.pallas_call(functools.partial(moe_kernel, (rows, depth, width, experts...  132 us
    unnamed x2, local copies, waits for them, and re-layouts  3.01 us

profile of v4, /device:TPU:91, one launch (start us, length us, event | category | flops | bytes accessed | tf_op | source)
XLA Modules:
  0.0 135.9 jit_solution(2116969539831553186)
XLA Ops:
  0.6 132.2 %shard_map.77 = (bf16[64,3584]{1,0:T(8,128)(2,1)}, f32[1,64]{1,0:T(1,128)}) custom-call(bf16[64,3584]{1,0:T(8,128)(2,1)} %tokens_ref.1, s32[8,64]{1,0:T(8,128)} %bitcast.4, bf16[64,3584]{1,0:T(8,128)(2,1)} %bitcast.3, bf16[1,3584,1024]{2,1,0:T(8,128)(2,1)} %wg_hbm.1, bf16[1,3584,1024]{2,1,0:T(8,128)(2,1)} %wu_hbm.1, bf16[1,1024,3584]{2,1,0:T(8,128)(2,1)} %wd_hbm.1), custom_call_target="tpu_custom_call" | custom-call | tf_op jit(solution)/shard_map/pallas_call | solution.py:496
  132.9 1.8 %copy.10 = bf16[64,3584]{1,0:T(8,128)(2,1)} copy(bf16[64,3584]{1,0:T(8,128)(2,1)} %get-tuple-element.8) | data formatting | bytes 917504
  134.7 1.2 copy.11
